TPU v7x, 32 devices: a whole 2x2x4 slice. The times are simulated.
32 devices in a mesh: src: 8 (over z, y), att: 4 (over x, core).
Axes of the slice: x: 2, y: 2, z: 4, core: 2. Of those that a mesh axis runs over, the one named last changes fastest.
Arguments:
- astro: float32 [5, 4096], P(None, 'src'), may hold values from -6 to 6
- attitude: float32 [196608], P('att'), may hold values from -6 to 6
- spline_weights: bfloat16 [2048, 64, 128], P(('src', 'att')), may hold values from -0.75 to 0.75
- source_coeffs: bfloat16 [2048, 5, 128], P(('src', 'att')), may hold values from -2.5 to 2.5
- observations: float32 [2048, 128], P(('src', 'att')), may hold values from -12 to 12
- knot_start: int32 [2048], P(('src', 'att')), may hold values from 0 to 49088
- block_count: int32 [4, 32], P('att', 'src'), may hold values from 1 to 16, as said below
Outputs:
- astro_new: float32 [5, 4096], P(None, 'src')
- attitude_new: float32 [196608], P('att')
Inputs may be any that keep to these rules, and one draw needn't show every extreme that they name: `block_count`: A block's live tiles fill its slots 0 to count - 1 at that owner; the other slots hold entries that no output reads. Some block has all 16 slots live.
All inputs are finite; a program needn't handle non-finite values.
Results may differ from a plain program's by a relative error of at most 0.0003.
Values sent between devices are 32-bit elements; how exact they have to be, the bound alone decides.
A program may use at most 64 MiB of HBM per device.

v0:
```python
import jax
import jax.numpy as jnp
from jax import lax
from jax.sharding import PartitionSpec as P

PASSES = 2
damping = 1.0


def attitude_model(weights, window):
    return jnp.sum(weights.astype(jnp.float32) * window[..., None], axis=-2)


def source_model(coeffs, params):
    return jnp.sum(coeffs.astype(jnp.float32) * params, axis=-2)


def local(astro, attitude, spline_weights, source_coeffs, observations, knot_start, block_count):
    blocks = block_count.shape[1]
    param_count = astro.shape[0]
    block_rows = astro.shape[1] // blocks
    slot_count = spline_weights.shape[0] // blocks
    knot_count = spline_weights.shape[1]
    knot_att = attitude.shape[0]
    weights = spline_weights.reshape(blocks, slot_count, knot_count, block_rows)
    coeffs = source_coeffs.reshape(blocks, slot_count, param_count, block_rows)
    observed = observations.reshape(blocks, slot_count, block_rows)
    starts = knot_start.reshape(blocks, slot_count)
    counts = block_count[0]
    tile_data = (weights, coeffs, observed, starts)
    offsets = jnp.arange(knot_count, dtype=jnp.int32)

    def over_slots(step_fn, totals):
        return step_fn(totals, tile_data, 0)

    def live_mask(slot_first, width):
        slot_ids = slot_first + jnp.arange(width, dtype=jnp.int32)
        return (slot_ids[None, :] < counts[:, None]).astype(jnp.float32)

    def residual(tile_part, slot_first, params, attitude_now):
        part_w, part_c, part_y, part_s = tile_part
        live = live_mask(slot_first, part_w.shape[1])
        window = attitude_now[part_s[..., None] + offsets]
        predicted = source_model(part_c, params[:, None]) + attitude_model(part_w, window)
        return (part_y - predicted) * live[..., None]

    def diag_step(totals, tile_part, slot_first):
        part_w, part_c, part_y, part_s = tile_part
        live = live_mask(slot_first, part_w.shape[1])
        source_sq = jnp.sum(jnp.square(part_c.astype(jnp.float32)) * live[:, :, None, None], axis=1)
        knot_sq = jnp.sum(jnp.square(part_w.astype(jnp.float32)), axis=-1) * live[:, :, None]
        return (source_sq, totals[1].at[part_s[..., None] + offsets].add(knot_sq))

    source_zero = jnp.zeros((blocks, param_count, block_rows), jnp.float32)
    knot_zero = jnp.zeros((knot_att,), jnp.float32)
    source_part, knot_part = over_slots(diag_step, (source_zero, knot_zero))
    source_diag = lax.psum(source_part, "att") + damping
    knot_diag = lax.psum(knot_part, "src") + damping
    params = jnp.transpose(astro.reshape(param_count, blocks, block_rows), (1, 0, 2))
    attitude_now = attitude
    for pass_no in range(PASSES):
        params_old = params
        attitude_old = attitude_now

        def source_step(totals, tile_part, slot_first):
            resid = residual(tile_part, slot_first, params_old, attitude_old)
            return jnp.sum(tile_part[1].astype(jnp.float32) * resid[:, :, None, :], axis=1)

        gradient = over_slots(source_step, source_zero)
        gradient = lax.psum(gradient, "att")
        params = params_old + gradient / source_diag
        params_new = params

        def knot_step(totals, tile_part, slot_first):
            resid = residual(tile_part, slot_first, params_new, attitude_old)
            values = jnp.sum(tile_part[0].astype(jnp.float32) * resid[:, :, None, :], axis=-1)
            return totals.at[tile_part[3][..., None] + offsets].add(values)

        knot_terms = over_slots(knot_step, knot_zero)
        knot_terms = lax.psum(knot_terms, "src")
        attitude_now = attitude_old + knot_terms / knot_diag
    astro_new = jnp.transpose(params, (1, 0, 2)).reshape(param_count, blocks * block_rows)
    return (astro_new, attitude_now)


def solution(mesh):
    placed = (
        P(None, "src"),
        P("att"),
        P(("src", "att"), None, None),
        P(("src", "att"), None, None),
        P(("src", "att"), None),
        P(("src", "att")),
        P("att", "src"),
    )
    return jax.shard_map(
        local, mesh=mesh, in_specs=placed, out_specs=(P(None, "src"), P("att")), check_vma=False
    )
```

profile of v0, /device:TPU:0, one launch (start us, length us, event | category | flops | bytes accessed | tf_op | source)
XLA Modules:
  0.0 318.1 jit_solution(2408341965380640918)
XLA Ops:
  7.2 0.7 fusion.14
  7.9 0.1 reshape.180
  8.0 0.7 add.83
  8.8 0.7 reshape.177
  9.7 19.6 %gather_fusion = f32[4096]{0:T(1024)S(1)} fusion(f32[49152]{0:T(1024)} %param.8, s32[4096]{0:T(1024)S(1)} %broadcast_clamp_fusion), kind=kCustom, calls=%fused_computation | custom fusion | bytes 49152 | tf_op jit(solution)/shard_map/gather | solution.py:43
  29.3 0.7 fusion
  30.0 0.1 copy-done.2
  30.3 0.1 multiply_reduce_fusion.1
  30.4 12.8 %all-reduce.1 = (f32[4,5,128]{2,0,1:T(4,128)S(1)}, f32[4,5,128]{2,0,1:T(4,128)S(1)}) all-reduce(f32[4,5,128]{2,0,1:T(4,128)S(1)} %get-tuple-element.5, f32[4,5,128]{2,0,1:T(4,128)S(1)} %get-tuple-element.4), channel_id=1, replica_groups=mesh['src'=8,'att'=4] {'att'}, use_global_device_ids=true, to_apply=%region_3.0 | all-reduce | flops 5120 | bytes 40960 | tf_op jit(solution)/shard_map/psum | solution.py:70
  43.2 0.1 subtract_multiply_fusion.1
  43.3 1.2 fusion.2
  44.7 29.2 %scatter_custom_fusion = f32[49152]{0:T(1024)} fusion(s32[4096]{0:T(1024)S(1)} %reshape.183, f32[4096]{0:T(1024)S(1)} %reshape.201, f32[]{:T(128)} %constant.4.clone.1), kind=kCustom, calls=%fused_computation.30 | custom fusion | flops 4096 | bytes 196612 | tf_op jit(solution)/shard_map/scatter-add | solution.py:77
  73.9 29.2 %scatter_custom_fusion.1 = f32[49152]{0:T(1024)} fusion(s32[4096]{0:T(1024)S(1)} %reshape.183, f32[4096]{0:T(1024)S(1)} %reshape.209, f32[]{:T(128)} %constant.4.clone.1), kind=kCustom, calls=%fused_computation.28 | custom fusion | flops 4096 | bytes 196612 | tf_op jit(solution)/shard_map/scatter-add | solution.py:52
  103.2 71.9 %all-reduce.7.cloned.1.call-done = (f32[49152]{0:T(1024)}, f32[49152]{0:T(1024)}) async-done(((f32[49152]{0:T(1024)}, f32[49152]{0:T(1024)}), (f32[49152]{0:T(1024)}, f32[49152]{0:T(1024)})) %all-reduce.7.cloned.1.call-update) | async-done | bytes 393232 | tf_op jit(solution)/shard_map/psum | solution.py:80
  175.1 1.1 divide_add_fusion.1
  176.1 23.0 %gather_fusion.1 = f32[4096]{0:T(1024)S(1)} fusion(f32[49152]{0:T(1024)S(1)} %divide_add_fusion.1, s32[4096]{0:T(1024)S(1)} %broadcast_clamp_fusion), kind=kCustom, calls=%fused_computation.1 | custom fusion | bytes 49152 | tf_op jit(solution)/shard_map/gather | solution.py:43
  199.3 0.7 fusion.3
  200.1 10.1 %psum.46 = f32[4,5,128]{2,0,1:T(4,128)S(1)} all-reduce(f32[4,5,128]{2,0,1:T(4,128)S(1)} %multiply_reduce_fusion), channel_id=1, replica_groups=mesh['src'=8,'att'=4] {'att'}, use_global_device_ids=true, to_apply=%region_15.0 | all-reduce | flops 2560 | bytes 20480 | tf_op jit(solution)/shard_map/psum | solution.py:70
  210.3 0.1 subtract_multiply_fusion
  210.4 0.6 fusion.4
  211.0 29.2 %scatter_custom_fusion.2 = f32[49152]{0:T(1024)} fusion(s32[4096]{0:T(1024)S(1)} %reshape.183, f32[4096]{0:T(1024)S(1)} %reshape.217, f32[]{:T(128)} %constant.4.clone.1), kind=kCustom, calls=%fused_computation.26 | custom fusion | flops 4096 | bytes 196612 | tf_op jit(solution)/shard_map/scatter-add | solution.py:77
  240.3 0.6 copy.11
  240.9 68.7 %all-reduce.5.cloned.1.call-done = f32[49152]{0:T(1024)} async-done(((f32[49152]{0:T(1024)}), f32[49152]{0:T(1024)}) %all-reduce.5.cloned.1.call-update) | async-done | bytes 196624 | tf_op jit(solution)/shard_map/psum | solution.py:80
  309.6 1.6 divide_add_fusion
  (32 shorter events, 1.0 us)
Async XLA Ops:
  7.2 167.9 %all-reduce.7.cloned.1.call-start = ((), (), s32[]{:S(2)}) async-start(), calls=%async_computation.1 | async-start | bytes 786432 | tf_op jit(solution)/shard_map/psum | solution.py:80
  9.6 19.7 %copy-start.1 = (bf16[64,64,128]{2,1,0:T(8,128)(2,1)S(1)}, bf16[64,64,128]{2,1,0:T(8,128)(2,1)}, u32[]{:S(2)}) copy-start(bf16[64,64,128]{2,1,0:T(8,128)(2,1)} %param.9) | copy-start | bytes 3145732
  29.2 0.9 copy-start.2
  29.3 0.9 copy-start.4
  43.3 131.8 %copy-start = (f32[49152]{0:T(1024)S(1)}, f32[49152]{0:T(1024)}, u32[]{:S(2)}) copy-start(f32[49152]{0:T(1024)} %param.8) | copy-start | bytes 589828
  103.2 206.4 %all-reduce.5.cloned.1.call-start = ((), (), s32[]{:S(2)}) async-start(), calls=%async_computation | async-start | bytes 393216 | tf_op jit(solution)/shard_map/psum | solution.py:80
  200.0 109.6 %copy-start.3 = (f32[49152]{0:T(1024)S(1)}, f32[49152]{0:T(1024)}, u32[]{:S(2)}) copy-start(f32[49152]{0:T(1024)} %get-tuple-element.7) | copy-start | bytes 589828
Sparse Core Ops, SparseCore 0:
  103.3 71.7 all-reduce.6
  240.4 69.1 all-reduce.4
where the time goes:
time: 318 us
  waiting for transfers between devices  141 us (44%)
  other arithmetic  95 us (30%)
  local copies, waits for them, and re-layouts  45.3 us (14%)
  blocking collectives  22.9 us (7%)
  between operations  14.2 us (4%)
    psum x2, waiting for transfers between devices, local(): knot_terms = lax.psum(knot_terms, 'src')  141 us
    scatter-add x2, other arithmetic, knot_step(): return totals.at[tile_part[3][..., None] + offsets].add(values)  58.5 us
    gather x2, local copies, waits for them, and re-layouts, residual(): window = attitude_now[part_s[..., None] + offsets]  42.6 us
    scatter-add x1, other arithmetic, diag_step(): return (source_sq, totals[1].at[part_s[..., None] + offsets].add(knot_sq))  29.2 us
    psum x2, blocking collectives, local(): gradient = lax.psum(gradient, 'att')  22.9 us
  transfers between devices with their start and end apart: 2, of which 2 were waited for; matrix products, arithmetic and copies ran while one was open for 0% of the time, Pallas kernels for 0%

commit v1 on v0

--- a/solution.py
+++ b/solution.py
@@ -67,7 +67,11 @@
             return jnp.sum(tile_part[1].astype(jnp.float32) * resid[:, :, None, :], axis=1)
 
         gradient = over_slots(source_step, source_zero)
-        gradient = lax.psum(gradient, "att")
+        gradient = gradient
+        for hop in (1, 2):
+            gradient = gradient + lax.ppermute(
+                gradient, "att", [(dev, dev ^ hop) for dev in range(4)]
+            )
         params = params_old + gradient / source_diag
         params_new = params
 

time: 318 us -> 316 us (level)
  blocking collectives: 22.9 us -> 10.1 us
  waiting for transfers between devices: 141 us -> 146 us
  starting transfers between devices: 0.08 us -> 4.86 us
    psum x2 -> x1, blocking collectives: 22.9 us -> 10.1 us  [local(): source_diag = lax.psum(source_part, 'att') + damping]
    ppermute x0 -> x4, starting transfers between devices: none -> 4.78 us  [local(): lax.ppermute(gradient, 'att', [(dev, dev ^ hop) for dev in range(4)])]
    ppermute x0 -> x4, waiting for transfers between devices: none -> 4.22 us  [local(): lax.ppermute(gradient, 'att', [(dev, dev ^ hop) for dev in range(4)])]
  transfers between devices with their start and end apart: 2 -> 6, of which waited for: 2 -> 5; matrix products, arithmetic and copies ran while one was open for 0% -> 0% of each run, Pallas kernels for 0% -> 0%
where the time goes in v1:
time: 316 us; the launch traced here: 315 us
  waiting for transfers between devices  146 us (46%)
  other arithmetic  95 us (30%)
  local copies, waits for them, and re-layouts  45.3 us (14%)
  between operations  14.2 us (4%)
  blocking collectives  10.1 us (3%)
  starting transfers between devices  4.86 us (2%)
    psum x2, waiting for transfers between devices, local(): knot_terms = lax.psum(knot_terms, 'src')  142 us
    scatter-add x2, other arithmetic, knot_step(): return totals.at[tile_part[3][..., None] + offsets].add(values)  58.5 us
    gather x2, local copies, waits for them, and re-layouts, residual(): window = attitude_now[part_s[..., None] + offsets]  42.6 us
    scatter-add x1, other arithmetic, diag_step(): return (source_sq, totals[1].at[part_s[..., None] + offsets].add(knot_sq))  29.2 us
    psum x1, blocking collectives, local(): source_diag = lax.psum(source_part, 'att') + damping  10.1 us
  transfers between devices with their start and end apart: 6, of which 5 were waited for; matrix products, arithmetic and copies ran while one was open for 0% of the time, Pallas kernels for 0%

profile of v1, /device:TPU:0, one launch (start us, length us, event | category | flops | bytes accessed | tf_op | source)
XLA Modules:
  0.0 315.2 jit_solution(2229550229278217061)
XLA Ops:
  7.2 0.7 fusion.14
  7.9 0.7 add.160
  8.7 0.7 reshape.177
  9.6 19.6 %gather_fusion = f32[4096]{0:T(1024)S(1)} fusion(f32[49152]{0:T(1024)} %param.8, s32[4096]{0:T(1024)S(1)} %broadcast_clamp_fusion), kind=kCustom, calls=%fused_computation | custom fusion | bytes 49152 | tf_op jit(solution)/shard_map/gather | solution.py:43
  29.3 0.7 fusion
  30.3 0.5 collective-permute-start
  30.9 0.7 collective-permute-done
  31.6 2.8 collective-permute-start.1
  34.5 10.1 %psum.28 = f32[4,5,128]{2,0,1:T(4,128)S(1)} all-reduce(f32[4,5,128]{2,0,1:T(4,128)S(1)} %get-tuple-element.4), channel_id=1, replica_groups=mesh['src'=8,'att'=4] {'att'}, use_global_device_ids=true, to_apply=%region_4.0 | all-reduce | flops 2560 | bytes 20480 | tf_op jit(solution)/shard_map/psum | solution.py:57
  44.7 1.2 fusion.2
  46.1 29.2 %scatter_custom_fusion = f32[49152]{0:T(1024)} fusion(s32[4096]{0:T(1024)S(1)} %reshape.183, f32[4096]{0:T(1024)S(1)} %reshape.201, f32[]{:T(128)} %constant.4.clone.1), kind=kCustom, calls=%fused_computation.30 | custom fusion | flops 4096 | bytes 196612 | tf_op jit(solution)/shard_map/scatter-add | solution.py:81
  75.3 29.2 %scatter_custom_fusion.1 = f32[49152]{0:T(1024)} fusion(s32[4096]{0:T(1024)S(1)} %reshape.183, f32[4096]{0:T(1024)S(1)} %reshape.209, f32[]{:T(128)} %constant.4.clone.1), kind=kCustom, calls=%fused_computation.28 | custom fusion | flops 4096 | bytes 196612 | tf_op jit(solution)/shard_map/scatter-add | solution.py:52
  104.6 72.9 %all-reduce.6.cloned.1.call-done = (f32[49152]{0:T(1024)}, f32[49152]{0:T(1024)}) async-done(((f32[49152]{0:T(1024)}, f32[49152]{0:T(1024)}), (f32[49152]{0:T(1024)}, f32[49152]{0:T(1024)})) %all-reduce.6.cloned.1.call-update) | async-done | bytes 393232 | tf_op jit(solution)/shard_map/psum | solution.py:84
  177.5 1.1 divide_add_fusion.1
  178.5 23.0 %gather_fusion.1 = f32[4096]{0:T(1024)S(1)} fusion(f32[49152]{0:T(1024)S(1)} %divide_add_fusion.1, s32[4096]{0:T(1024)S(1)} %broadcast_clamp_fusion), kind=kCustom, calls=%fused_computation.1 | custom fusion | bytes 49152 | tf_op jit(solution)/shard_map/gather | solution.py:43
  201.6 0.7 fusion.3
  202.6 1.2 collective-permute-done.2
  203.7 1.4 collective-permute-start.3
  205.1 2.3 collective-permute-done.3
  207.5 0.6 fusion.4
  208.2 29.2 %scatter_custom_fusion.2 = f32[49152]{0:T(1024)} fusion(s32[4096]{0:T(1024)S(1)} %reshape.183, f32[4096]{0:T(1024)S(1)} %reshape.217, f32[]{:T(128)} %constant.4.clone.1), kind=kCustom, calls=%fused_computation.26 | custom fusion | flops 4096 | bytes 196612 | tf_op jit(solution)/shard_map/scatter-add | solution.py:81
  237.5 0.6 copy.11
  238.1 68.7 %all-reduce.4.cloned.1.call-done = f32[49152]{0:T(1024)} async-done(((f32[49152]{0:T(1024)}), f32[49152]{0:T(1024)}) %all-reduce.4.cloned.1.call-update) | async-done | bytes 196624 | tf_op jit(solution)/shard_map/psum | solution.py:84
  306.8 1.6 divide_add_fusion
  (41 shorter events, 1.5 us)
Async XLA Ops:
  7.2 170.3 %all-reduce.6.cloned.1.call-start = ((), (), s32[]{:S(2)}) async-start(), calls=%async_computation.1 | async-start | bytes 786432 | tf_op jit(solution)/shard_map/psum | solution.py:84
  9.6 19.7 %copy-start.1 = (bf16[64,64,128]{2,1,0:T(8,128)(2,1)S(1)}, bf16[64,64,128]{2,1,0:T(8,128)(2,1)}, u32[]{:S(2)}) copy-start(bf16[64,64,128]{2,1,0:T(8,128)(2,1)} %param.9) | copy-start | bytes 3145732
  29.2 0.9 copy-start.2
  29.2 0.9 copy-start.4
  30.3 1.4 collective-permute-start
  31.6 12.9 %collective-permute-start.1 = (f32[4,5,128]{2,0,1:T(4,128)S(1)}, f32[4,5,128]{2,0,1:T(4,128)S(1)}, u32[]{:S(2)}, u32[]{:S(2)}) collective-permute-start(f32[4,5,128]{2,0,1:T(4,128)S(1)} %add.166), channel_id=1, source_target_pairs={{0,2},{1,3},{2,0},{3,1},{4,6},{5,7},{6,4},{7,5},{8,10},{9,11},{10,... | collective-permute-start | bytes 30728 | tf_op jit(solution)/shard_map/ppermute | solution.py:72
  44.7 132.8 %copy-start = (f32[49152]{0:T(1024)S(1)}, f32[49152]{0:T(1024)}, u32[]{:S(2)}) copy-start(f32[49152]{0:T(1024)} %param.8) | copy-start | bytes 589828
  104.6 202.2 %all-reduce.4.cloned.1.call-start = ((), (), s32[]{:S(2)}) async-start(), calls=%async_computation | async-start | bytes 393216 | tf_op jit(solution)/shard_map/psum | solution.py:84
  202.4 104.4 %copy-start.3 = (f32[49152]{0:T(1024)S(1)}, f32[49152]{0:T(1024)}, u32[]{:S(2)}) copy-start(f32[49152]{0:T(1024)} %get-tuple-element.7) | copy-start | bytes 589828
  202.5 1.2 collective-permute-start.2
  203.7 3.7 %collective-permute-start.3 = (f32[4,5,128]{2,0,1:T(4,128)S(1)}, f32[4,5,128]{2,0,1:T(4,128)S(1)}, u32[]{:S(2)}, u32[]{:S(2)}) collective-permute-start(f32[4,5,128]{2,0,1:T(4,128)S(1)} %add.176), channel_id=1, source_target_pairs={{0,2},{1,3},{2,0},{3,1},{4,6},{5,7},{6,4},{7,5},{8,10},{9,11},{10,... | collective-permute-start | bytes 30728 | tf_op jit(solution)/shard_map/ppermute | solution.py:72
Sparse Core Ops, SparseCore 0:
  104.7 72.7 all-reduce.5
  237.6 69.1 all-reduce.3
